TPU v7x, 32 devices: a whole 2x2x4 slice. The times are simulated.
32 devices in a mesh: groups: 2 (over y), tm: 4 (over z), fibre: 4 (over x, core).
Axes of the slice: x: 2, y: 2, z: 4, core: 2. Of those that a mesh axis runs over, the one named last changes fastest.
Arguments:
- recording: bfloat16 [256, 128, 256], P(('groups', 'tm'), 'fibre'), parts along dimension 0, may hold values from -6 to 6
- conv_weight: bfloat16 [2, 3, 3, 256, 512], replicated, may hold values from -0.125 to 0.125
- conv_bias: float32 [2, 512], replicated, may hold values from -0.5 to 0.5
- res_weight: bfloat16 [2, 256, 256], replicated, may hold values from -0.375 to 0.375
- skip_weight: bfloat16 [2, 256, 256], replicated, may hold values from -0.375 to 0.375
- head_weight: bfloat16 [256, 1024], replicated, may hold values from -0.375 to 0.375
Outputs:
- residual_out: bfloat16 [256, 128, 256], P(('groups', 'tm'), 'fibre'), parts along dimension 0
- denoised: bfloat16 [256, 128, 1024], P(('groups', 'tm'), 'fibre'), parts along dimension 0
There are 2 independent parts, one for each index of `groups`. A program takes and returns all parts, laid end to end along the dimension named above; an argument that names none is the same for every part. Nothing has to cross between parts.
All inputs are finite; a program needn't handle non-finite values.
Results may differ from a plain program's by a relative error of at most 0.0062.
Values may be sent and summed in bfloat16 or wider, within the bound.
A program may use at most 64 MiB of HBM per device.

v0:
```python
import jax
import jax.numpy as jnp
from jax import lax
from jax.sharding import PartitionSpec as P

DILATION_SPAN = 32


def passed_along(shard, axis, by):
    devices = lax.axis_size(axis)
    pairs = [(i, i + by) for i in range(devices) if 0 <= i + by < devices]
    return lax.ppermute(shard, axis, pairs)


def padded(block, sides, width):
    for axis, dim in sides:
        count = lax.axis_size(axis)
        forward = [(i, i + 1) for i in range(count - 1)]
        backward = [(target, source) for source, target in forward]
        low = lax.ppermute(
            lax.slice_in_dim(block, block.shape[dim] - width, None, axis=dim), axis, forward
        )
        high = lax.ppermute(lax.slice_in_dim(block, 0, width, axis=dim), axis, backward)
        block = jnp.concatenate([low, block, high], axis=dim)
    return block


def gate_layer(earlier, middle, later, layer_weight, layer_bias):
    channels = middle.shape[-1]
    fibre_rows = middle.shape[-2] - 2
    summed = None
    for time_offset, block in enumerate((earlier, middle, later)):
        for fibre_offset in range(3):
            receptive_view = block[..., fibre_offset : fibre_offset + fibre_rows, :].reshape(
                -1, channels
            )
            product = jnp.dot(
                receptive_view,
                layer_weight[time_offset, fibre_offset],
                preferred_element_type=jnp.float32,
            )
            summed = product if summed is None else summed + product
    before_gate = summed + layer_bias
    return (jnp.tanh(before_gate[:, :channels]) * jax.nn.sigmoid(before_gate[:, channels:])).astype(
        jnp.bfloat16
    )


def update(gated, stream_rows, skipped, layer_res, layer_skip):
    new_stream = (
        stream_rows.astype(jnp.float32)
        + jnp.dot(gated, layer_res, preferred_element_type=jnp.float32)
    ).astype(jnp.bfloat16)
    new_skip = skipped + jnp.dot(gated, layer_skip, preferred_element_type=jnp.float32)
    return (new_stream, new_skip)


def head_out(skipped, head_weight):
    rectified = jnp.maximum(skipped, 0.0).astype(jnp.bfloat16)
    return jnp.dot(rectified, head_weight, preferred_element_type=jnp.float32).astype(jnp.bfloat16)


def local(recording, conv_weight, conv_bias, res_weight, skip_weight, head_weight):
    time_slices, strips, channels = recording.shape
    layer_count = conv_weight.shape[0]
    stream = recording
    skipped = jnp.zeros((time_slices * strips, channels), jnp.float32)
    for layer in range(layer_count):
        tap_spacing = DILATION_SPAN * 2**layer // time_slices
        earlier_bare = passed_along(stream, "tm", tap_spacing)
        later_bare = passed_along(stream, "tm", -tap_spacing)
        stacked = jnp.stack([earlier_bare, stream, later_bare])
        border_filled = padded(stacked, (("fibre", 2),), 1)
        earlier, middle, later = (border_filled[0], border_filled[1], border_filled[2])
        gated = gate_layer(earlier, middle, later, conv_weight[layer], conv_bias[layer])
        new_rows, skipped = update(
            gated, stream.reshape(-1, channels), skipped, res_weight[layer], skip_weight[layer]
        )
        stream = new_rows.reshape(time_slices, strips, channels)
    denoised = head_out(skipped, head_weight)
    return (stream, denoised.reshape(time_slices, strips, -1))


def solution(mesh):
    return jax.shard_map(
        local,
        mesh=mesh,
        in_specs=(P(("groups", "tm"), "fibre", None), P(), P(), P(), P(), P()),
        out_specs=(P(("groups", "tm"), "fibre", None), P(("groups", "tm"), "fibre", None)),
        check_vma=False,
    )
```

profile of v0, /device:TPU:1, one launch (start us, length us, event | category | flops | bytes accessed | tf_op | source)
XLA Modules:
  0.0 86.6 jit_solution(2297417337786201158)
XLA Ops:
  0.6 0.0 copy-start
  0.6 0.0 copy-start.1
  0.7 0.0 copy-start.4
  0.7 4.2 %collective-permute-start = (bf16[32,32,256]{2,1,0:T(8,128)(2,1)}, bf16[32,32,256]{2,1,0:T(8,128)(2,1)S(1)}, u32[]{:S(2)}, u32[]{:S(2)}) collective-permute-start(bf16[32,32,256]{2,1,0:T(8,128)(2,1)} %param.6), channel_id=1, source_target_pairs={{0,4},{4,8},{8,12},{1,5},{5,9},{9,13},{2,6},{6,10},{10,14},{3,7},{... | collective-permute-start | bytes 1572872 | tf_op jit(solution)/shard_map/ppermute | solution.py:12
  4.9 1.3 %collective-permute-start.1 = (bf16[32,32,256]{2,1,0:T(8,128)(2,1)}, bf16[32,32,256]{2,1,0:T(8,128)(2,1)S(1)}, u32[]{:S(2)}, u32[]{:S(2)}) collective-permute-start(bf16[32,32,256]{2,1,0:T(8,128)(2,1)} %param.6), channel_id=1, source_target_pairs={{4,0},{8,4},{12,8},{5,1},{9,5},{13,9},{6,2},{10,6},{14,10},{7,3},{... | collective-permute-start | bytes 1572872 | tf_op jit(solution)/shard_map/ppermute | solution.py:12
  6.2 2.8 %slice_bitcast_fusion = (bf16[3,3,256,512]{3,2,1,0:T(8,128)(2,1)S(1)}, bf16[3,3,256,512]{3,2,1,0:T(8,128)(2,1)S(1)}) fusion(bf16[2,3,3,256,512]{4,3,2,1,0:T(8,128)(2,1)} %param.7), kind=kLoop, calls=%fused_computation | loop fusion | bytes 9437184 | tf_op jit(solution)/shard_map/squeeze | solution.py:75
  9.0 6.7 %collective-permute-done = bf16[32,32,256]{2,1,0:T(8,128)(2,1)S(1)} collective-permute-done((bf16[32,32,256]{2,1,0:T(8,128)(2,1)}, bf16[32,32,256]{2,1,0:T(8,128)(2,1)S(1)}, u32[]{:S(2)}, u32[]{:S(2)}) %collective-permute-start) | collective-permute-done | bytes 524320 | tf_op jit(solution)/shard_map/ppermute | solution.py:12
  15.7 3.7 %collective-permute-done.1 = bf16[32,32,256]{2,1,0:T(8,128)(2,1)S(1)} collective-permute-done((bf16[32,32,256]{2,1,0:T(8,128)(2,1)}, bf16[32,32,256]{2,1,0:T(8,128)(2,1)S(1)}, u32[]{:S(2)}, u32[]{:S(2)}) %collective-permute-start.1) | collective-permute-done | bytes 524320 | tf_op jit(solution)/shard_map/ppermute | solution.py:12
  19.4 0.0 copy-done.1
  19.4 0.2 pad_maximum_fusion.7
  19.6 4.9 %collective-permute-start.2 = (bf16[3,32,1,256]{3,2,1,0:T(2,128)(2,1)S(1)}, bf16[3,32,1,256]{3,2,1,0:T(2,128)(2,1)S(1)}, u32[]{:S(2)}, u32[]{:S(2)}) collective-permute-start(bf16[3,32,1,256]{3,2,1,0:T(2,128)(2,1)S(1)} %get-tuple-element.12), channel_id=1, source_target_pairs={{0,1},{1,2},{2,3},{4,5},{5,6},{6,7},{8,9},{9,10},{10,11},{12,13},{... | collective-permute-start | bytes 147464 | tf_op jit(solution)/shard_map/ppermute | solution.py:20
  24.5 1.9 %collective-permute-start.3 = (bf16[3,32,1,256]{3,2,1,0:T(2,128)(2,1)S(1)}, bf16[3,32,1,256]{3,2,1,0:T(2,128)(2,1)S(1)}, u32[]{:S(2)}, u32[]{:S(2)}) collective-permute-start(bf16[3,32,1,256]{3,2,1,0:T(2,128)(2,1)S(1)} %get-tuple-element.13), channel_id=1, source_target_pairs={{1,0},{2,1},{3,2},{5,4},{6,5},{7,6},{9,8},{10,9},{11,10},{13,12},{... | collective-permute-start | bytes 147464 | tf_op jit(solution)/shard_map/ppermute | solution.py:23
  26.4 0.0 copy-done.4
  26.4 0.0 collective-permute-done.2
  26.4 4.0 %collective-permute-done.3 = bf16[3,32,1,256]{3,2,1,0:T(2,128)(2,1)S(1)} collective-permute-done((bf16[3,32,1,256]{3,2,1,0:T(2,128)(2,1)S(1)}, bf16[3,32,1,256]{3,2,1,0:T(2,128)(2,1)S(1)}, u32[]{:S(2)}, u32[]{:S(2)}) %collective-permute-start.3) | collective-permute-done | bytes 49184 | tf_op jit(solution)/shard_map/ppermute | solution.py:23
  30.4 1.3 %pad_maximum_fusion = bf16[3,32,34,256]{3,2,1,0:T(8,128)(2,1)S(1)} fusion(bf16[3,32,1,256]{3,2,1,0:T(2,128)(2,1)S(1)} %collective-permute-done.3, bf16[1,32,32,256]{3,2,1,0:T(8,128)(2,1)S(1)} %bitcast.147, bf16[1,32,32,256]{3,2,1,0:T(8,128)(2,1)S(1)} %bitcast.142, bf16[1,32,32,256]{3,2,1,0:T(8,128)(2,1)S(1)} %bitcast.145, ...), kind=kLoop, calls=%fused_computation.4 | loop fusion | flops 8355840 | bytes 3342336 | tf_op jit(solution)/shard_map/concatenate | solution.py:24
  31.7 0.1 slice_bitcast_fusion.7
  31.8 0.8 fusion.46
  32.6 0.4 fusion.23
  33.0 0.4 fusion.24
  33.5 0.4 fusion.28
  33.9 0.4 fusion.29
  34.3 0.4 fusion.30
  34.7 0.4 fusion.48
  35.1 0.4 fusion.25
  35.5 0.4 fusion.26
  36.0 0.4 fusion.27
  36.4 1.0 %add_add_fusion.1 = f32[1024,512]{1,0:T(8,128)S(1)} fusion(f32[1024,512]{1,0:T(8,128)S(1)} %fusion.23, f32[1024,512]{1,0:T(8,128)S(1)} %fusion.24, f32[1024,512]{1,0:T(8,128)S(1)} %fusion.25, f32[1024,512]{1,0:T(8,128)S(1)} %fusion.26, f32[1024,512]{1,0:T(8,128)S(1)} %fusion.27, f32[1024,512]{1,0:T(8,128)S(1)} %fusion.28, f32[1024,512]{1,0:T(8,128)S(1)} %fusion.30, ...), kind=kOutput, calls=%fused_computation.3 | convolution fusion | flops 273154048 | bytes 19662848 | tf_op jit(solution)/shard_map/dot_general | solution.py:37
  37.4 0.0 copy-start.3
  37.4 0.4 fusion.12
  37.8 0.0 copy-start.2
  37.8 0.5 copy-done.3
  38.3 0.3 fusion.2
  38.6 4.3 %collective-permute-start.4 = (bf16[32,32,256]{2,1,0:T(8,128)(2,1)S(1)}, bf16[32,32,256]{2,1,0:T(8,128)(2,1)S(1)}, u32[]{:S(2)}, u32[]{:S(2)}) collective-permute-start(bf16[32,32,256]{2,1,0:T(8,128)(2,1)S(1)} %bitcast.137), channel_id=1, source_target_pairs={{0,8},{4,12},{1,9},{5,13},{2,10},{6,14},{3,11},{7,15},{16,24},{20,... | collective-permute-start | bytes 1572872 | tf_op jit(solution)/shard_map/ppermute | solution.py:12
  42.9 1.3 %collective-permute-start.5 = (bf16[32,32,256]{2,1,0:T(8,128)(2,1)S(1)}, bf16[32,32,256]{2,1,0:T(8,128)(2,1)S(1)}, u32[]{:S(2)}, u32[]{:S(2)}) collective-permute-start(bf16[32,32,256]{2,1,0:T(8,128)(2,1)S(1)} %bitcast.138), channel_id=1, source_target_pairs={{8,0},{12,4},{9,1},{13,5},{10,2},{14,6},{11,3},{15,7},{24,16},{28,... | collective-permute-start | bytes 1572872 | tf_op jit(solution)/shard_map/ppermute | solution.py:12
  44.2 8.2 %collective-permute-done.4 = bf16[32,32,256]{2,1,0:T(8,128)(2,1)S(1)} collective-permute-done((bf16[32,32,256]{2,1,0:T(8,128)(2,1)S(1)}, bf16[32,32,256]{2,1,0:T(8,128)(2,1)S(1)}, u32[]{:S(2)}, u32[]{:S(2)}) %collective-permute-start.4) | collective-permute-done | bytes 524320 | tf_op jit(solution)/shard_map/ppermute | solution.py:12
  52.4 15.4 %collective-permute-done.5 = bf16[32,32,256]{2,1,0:T(8,128)(2,1)S(1)} collective-permute-done((bf16[32,32,256]{2,1,0:T(8,128)(2,1)S(1)}, bf16[32,32,256]{2,1,0:T(8,128)(2,1)S(1)}, u32[]{:S(2)}, u32[]{:S(2)}) %collective-permute-start.5) | collective-permute-done | bytes 524320 | tf_op jit(solution)/shard_map/ppermute | solution.py:12
  67.8 0.2 pad_maximum_fusion.4
  68.0 1.9 %collective-permute-start.6 = (bf16[3,32,1,256]{3,2,1,0:T(2,128)(2,1)S(1)}, bf16[3,32,1,256]{3,2,1,0:T(2,128)(2,1)S(1)}, u32[]{:S(2)}, u32[]{:S(2)}) collective-permute-start(bf16[3,32,1,256]{3,2,1,0:T(2,128)(2,1)S(1)} %get-tuple-element.10), channel_id=1, source_target_pairs={{0,1},{1,2},{2,3},{4,5},{5,6},{6,7},{8,9},{9,10},{10,11},{12,13},{... | collective-permute-start | bytes 147464 | tf_op jit(solution)/shard_map/ppermute | solution.py:20
  69.9 2.6 %collective-permute-start.7 = (bf16[3,32,1,256]{3,2,1,0:T(2,128)(2,1)S(1)}, bf16[3,32,1,256]{3,2,1,0:T(2,128)(2,1)S(1)}, u32[]{:S(2)}, u32[]{:S(2)}) collective-permute-start(bf16[3,32,1,256]{3,2,1,0:T(2,128)(2,1)S(1)} %get-tuple-element.11), channel_id=1, source_target_pairs={{1,0},{2,1},{3,2},{5,4},{6,5},{7,6},{9,8},{10,9},{11,10},{13,12},{... | collective-permute-start | bytes 147464 | tf_op jit(solution)/shard_map/ppermute | solution.py:23
  72.5 0.0 copy-done.2
  72.5 0.3 fusion.33
  72.8 0.0 collective-permute-done.6
  72.8 3.0 %collective-permute-done.7 = bf16[3,32,1,256]{3,2,1,0:T(2,128)(2,1)S(1)} collective-permute-done((bf16[3,32,1,256]{3,2,1,0:T(2,128)(2,1)S(1)}, bf16[3,32,1,256]{3,2,1,0:T(2,128)(2,1)S(1)}, u32[]{:S(2)}, u32[]{:S(2)}) %collective-permute-start.7) | collective-permute-done | bytes 49184 | tf_op jit(solution)/shard_map/ppermute | solution.py:23
  75.9 1.3 %pad_maximum_fusion.1 = bf16[3,32,34,256]{3,2,1,0:T(8,128)(2,1)S(1)} fusion(bf16[3,32,1,256]{3,2,1,0:T(2,128)(2,1)S(1)} %collective-permute-done.7, bf16[1,32,32,256]{3,2,1,0:T(8,128)(2,1)S(1)} %bitcast.151, bf16[1,32,32,256]{3,2,1,0:T(8,128)(2,1)S(1)} %bitcast.140, bf16[1,32,32,256]{3,2,1,0:T(8,128)(2,1)S(1)} %bitcast.149, ...), kind=kLoop, calls=%fused_computation.5 | loop fusion | flops 8355840 | bytes 3342336 | tf_op jit(solution)/shard_map/concatenate | solution.py:24
  77.1 0.1 slice_bitcast_fusion.4
  77.3 0.4 fusion.45
  77.6 0.4 fusion.17
  78.1 0.4 fusion.18
  78.5 0.4 fusion.19
  78.9 0.4 fusion.44
  79.3 0.4 fusion.20
  79.7 0.4 fusion.21
  80.2 0.4 fusion.22
  80.6 0.4 fusion.43
  81.0 0.4 fusion.16
  81.4 0.4 fusion.15
  81.8 1.0 %add_add_fusion = f32[1024,512]{1,0:T(8,128)S(1)} fusion(f32[1024,512]{1,0:T(8,128)S(1)} %fusion.15, f32[1024,512]{1,0:T(8,128)S(1)} %fusion.16, f32[1024,512]{1,0:T(8,128)S(1)} %fusion.17, f32[1024,512]{1,0:T(8,128)S(1)} %fusion.18, f32[1024,512]{1,0:T(8,128)S(1)} %fusion.19, f32[1024,512]{1,0:T(8,128)S(1)} %fusion.20, f32[1024,512]{1,0:T(8,128)S(1)} %fusion.22, ...), kind=kOutput, calls=%fused_computation.2 | convolution fusion | flops 273154048 | bytes 19662848 | tf_op jit(solution)/shard_map/dot_general | solution.py:37
  82.8 0.4 fusion.13
  83.3 1.1 %fusion.3 = bf16[1024,256]{1,0:T(8,128)(2,1)} fusion(bf16[1024,256]{1,0:T(8,128)(2,1)S(1)} %fusion.13, bf16[1024,256]{1,0:T(8,128)(2,1)S(1)} %fusion.2, bf16[2,256,256]{2,1,0:T(8,128)(2,1)S(1)} %copy-done.3), kind=kOutput, calls=%fused_computation.13 | convolution fusion | flops 135004160 | bytes 1703936 | tf_op jit(solution)/shard_map/dot_general | solution.py:52
  84.4 0.0 copy-done
  84.4 2.2 %convolution_convert_fusion = bf16[1024,1024]{1,0:T(8,128)(2,1)} fusion(bf16[256,1024]{1,0:T(8,128)(2,1)S(1)} %copy-done, f32[1024,256]{1,0:T(8,128)S(1)} %fusion.33, bf16[1024,256]{1,0:T(8,128)(2,1)S(1)} %fusion.13, bf16[2,256,256]{2,1,0:T(8,128)(2,1)S(1)} %copy-done.2), kind=kOutput, calls=%fused_computation.6 | convolution fusion | flops 672923648 | bytes 4325376 | tf_op jit(solution)/shard_map/dot_general | solution.py:60
  (1 shorter events, 0.0 us)
Async XLA Ops:
  0.6 83.8 %copy-start = (bf16[256,1024]{1,0:T(8,128)(2,1)S(1)}, bf16[256,1024]{1,0:T(8,128)(2,1)}, u32[]{:S(2)}) copy-start(bf16[256,1024]{1,0:T(8,128)(2,1)} %param.11) | copy-start | bytes 1572868
  0.6 18.8 %copy-start.1 = (bf16[32,32,256]{2,1,0:T(8,128)(2,1)S(1)}, bf16[32,32,256]{2,1,0:T(8,128)(2,1)}, u32[]{:S(2)}) copy-start(bf16[32,32,256]{2,1,0:T(8,128)(2,1)} %param.6) | copy-start | bytes 1572868
  0.7 25.8 %copy-start.4 = (f32[2,512]{1,0:T(2,128)S(1)}, f32[2,512]{1,0:T(2,128)}, u32[]{:S(2)}) copy-start(f32[2,512]{1,0:T(2,128)} %param.8) | copy-start | bytes 12292
  0.7 15.1 %collective-permute-start = (bf16[32,32,256]{2,1,0:T(8,128)(2,1)}, bf16[32,32,256]{2,1,0:T(8,128)(2,1)S(1)}, u32[]{:S(2)}, u32[]{:S(2)}) collective-permute-start(bf16[32,32,256]{2,1,0:T(8,128)(2,1)} %param.6), channel_id=1, source_target_pairs={{0,4},{4,8},{8,12},{1,5},{5,9},{9,13},{2,6},{6,10},{10,14},{3,7},{... | collective-permute-start | bytes 1572872 | tf_op jit(solution)/shard_map/ppermute | solution.py:12
  4.9 14.6 %collective-permute-start.1 = (bf16[32,32,256]{2,1,0:T(8,128)(2,1)}, bf16[32,32,256]{2,1,0:T(8,128)(2,1)S(1)}, u32[]{:S(2)}, u32[]{:S(2)}) collective-permute-start(bf16[32,32,256]{2,1,0:T(8,128)(2,1)} %param.6), channel_id=1, source_target_pairs={{4,0},{8,4},{12,8},{5,1},{9,5},{13,9},{6,2},{10,6},{14,10},{7,3},{... | collective-permute-start | bytes 1572872 | tf_op jit(solution)/shard_map/ppermute | solution.py:12
  19.6 6.8 %collective-permute-start.2 = (bf16[3,32,1,256]{3,2,1,0:T(2,128)(2,1)S(1)}, bf16[3,32,1,256]{3,2,1,0:T(2,128)(2,1)S(1)}, u32[]{:S(2)}, u32[]{:S(2)}) collective-permute-start(bf16[3,32,1,256]{3,2,1,0:T(2,128)(2,1)S(1)} %get-tuple-element.12), channel_id=1, source_target_pairs={{0,1},{1,2},{2,3},{4,5},{5,6},{6,7},{8,9},{9,10},{10,11},{12,13},{... | collective-permute-start | bytes 147464 | tf_op jit(solution)/shard_map/ppermute | solution.py:20
  24.5 5.9 %collective-permute-start.3 = (bf16[3,32,1,256]{3,2,1,0:T(2,128)(2,1)S(1)}, bf16[3,32,1,256]{3,2,1,0:T(2,128)(2,1)S(1)}, u32[]{:S(2)}, u32[]{:S(2)}) collective-permute-start(bf16[3,32,1,256]{3,2,1,0:T(2,128)(2,1)S(1)} %get-tuple-element.13), channel_id=1, source_target_pairs={{1,0},{2,1},{3,2},{5,4},{6,5},{7,6},{9,8},{10,9},{11,10},{13,12},{... | collective-permute-start | bytes 147464 | tf_op jit(solution)/shard_map/ppermute | solution.py:23
  37.4 1.0 %copy-start.3 = (bf16[2,256,256]{2,1,0:T(8,128)(2,1)S(1)}, bf16[2,256,256]{2,1,0:T(8,128)(2,1)}, u32[]{:S(2)}) copy-start(bf16[2,256,256]{2,1,0:T(8,128)(2,1)} %param.9) | copy-start | bytes 786436
  37.8 34.7 %copy-start.2 = (bf16[2,256,256]{2,1,0:T(8,128)(2,1)S(1)}, bf16[2,256,256]{2,1,0:T(8,128)(2,1)}, u32[]{:S(2)}) copy-start(bf16[2,256,256]{2,1,0:T(8,128)(2,1)} %param.10) | copy-start | bytes 786436
  38.6 13.8 %collective-permute-start.4 = (bf16[32,32,256]{2,1,0:T(8,128)(2,1)S(1)}, bf16[32,32,256]{2,1,0:T(8,128)(2,1)S(1)}, u32[]{:S(2)}, u32[]{:S(2)}) collective-permute-start(bf16[32,32,256]{2,1,0:T(8,128)(2,1)S(1)} %bitcast.137), channel_id=1, source_target_pairs={{0,8},{4,12},{1,9},{5,13},{2,10},{6,14},{3,11},{7,15},{16,24},{20,... | collective-permute-start | bytes 1572872 | tf_op jit(solution)/shard_map/ppermute | solution.py:12
  42.9 24.9 %collective-permute-start.5 = (bf16[32,32,256]{2,1,0:T(8,128)(2,1)S(1)}, bf16[32,32,256]{2,1,0:T(8,128)(2,1)S(1)}, u32[]{:S(2)}, u32[]{:S(2)}) collective-permute-start(bf16[32,32,256]{2,1,0:T(8,128)(2,1)S(1)} %bitcast.138), channel_id=1, source_target_pairs={{8,0},{12,4},{9,1},{13,5},{10,2},{14,6},{11,3},{15,7},{24,16},{28,... | collective-permute-start | bytes 1572872 | tf_op jit(solution)/shard_map/ppermute | solution.py:12
  68.0 4.8 %collective-permute-start.6 = (bf16[3,32,1,256]{3,2,1,0:T(2,128)(2,1)S(1)}, bf16[3,32,1,256]{3,2,1,0:T(2,128)(2,1)S(1)}, u32[]{:S(2)}, u32[]{:S(2)}) collective-permute-start(bf16[3,32,1,256]{3,2,1,0:T(2,128)(2,1)S(1)} %get-tuple-element.10), channel_id=1, source_target_pairs={{0,1},{1,2},{2,3},{4,5},{5,6},{6,7},{8,9},{9,10},{10,11},{12,13},{... | collective-permute-start | bytes 147464 | tf_op jit(solution)/shard_map/ppermute | solution.py:20
  69.9 5.9 %collective-permute-start.7 = (bf16[3,32,1,256]{3,2,1,0:T(2,128)(2,1)S(1)}, bf16[3,32,1,256]{3,2,1,0:T(2,128)(2,1)S(1)}, u32[]{:S(2)}, u32[]{:S(2)}) collective-permute-start(bf16[3,32,1,256]{3,2,1,0:T(2,128)(2,1)S(1)} %get-tuple-element.11), channel_id=1, source_target_pairs={{1,0},{2,1},{3,2},{5,4},{6,5},{7,6},{9,8},{10,9},{11,10},{13,12},{... | collective-permute-start | bytes 147464 | tf_op jit(solution)/shard_map/ppermute | solution.py:23
where the time goes:
time: 86.9 us; the launch traced here: 86.6 us
  waiting for transfers between devices  41 us (47%)
  starting transfers between devices  22.4 us (26%)
  matrix products  12.7 us (15%)
  local copies, waits for them, and re-layouts  5.85 us (7%)
  other arithmetic  3.72 us (4%)
  between operations  0.9 us (1%)
    ppermute x4, waiting for transfers between devices, passed_along(): return lax.ppermute(shard, axis, pairs)  34 us
    ppermute x4, starting transfers between devices, passed_along(): return lax.ppermute(shard, axis, pairs)  11.1 us
    dot_general x18, matrix products, gate_layer(): jnp.dot(receptive_view, layer_weight[time_offset, fibre_offset], preferre...  8.83 us
    ppermute x2, waiting for transfers between devices, padded(): lax.ppermute(lax.slice_in_dim(block, 0, width, axis=dim), axis, backward)  6.99 us
    ppermute x2, starting transfers between devices, padded(): lax.ppermute(lax.slice_in_dim(block, block.shape[dim] - width, None, axis...  6.79 us
    ppermute x2, starting transfers between devices, padded(): lax.ppermute(lax.slice_in_dim(block, 0, width, axis=dim), axis, backward)  4.51 us
    squeeze x1, local copies, waits for them, and re-layouts, local(): conv_weight[layer]  2.84 us
    concatenate x2, other arithmetic, padded(): block = jnp.concatenate([low, block, high], axis=dim)  2.52 us
  transfers between devices with their start and end apart: 8, of which 6 were waited for; matrix products, arithmetic and copies ran while one was open for 4% of the time, Pallas kernels for 0%

commit v1 on v0

--- a/solution.py
+++ b/solution.py
@@ -1,6 +1,8 @@
 import jax
 import jax.numpy as jnp
 from jax import lax
+from jax.experimental import pallas as pl
+from jax.experimental.pallas import tpu as pltpu
 from jax.sharding import PartitionSpec as P
 
 DILATION_SPAN = 32
@@ -81,9 +83,332 @@
     return (stream, denoised.reshape(time_slices, strips, -1))
 
 
+MESH = pl.DeviceIdType.MESH
+M, O, I, F, S1M, S1F, S1I = range(7)
+HALF = 16
+
+
+def fused_kernel(x_ref, cw_hbm, cb_ref, rs_hbm, hd_hbm, res_ref, out_ref,
+                 buf, cw, rs, hd, skip, w_sem, send_sem, recv_sem, hsend, hrecv):
+    strips = x_ref.shape[1]
+    channels = x_ref.shape[2]
+    halves = x_ref.shape[0] // HALF
+    rows = HALF * strips
+    z = lax.axis_index("tm")
+    f = lax.axis_index("fibre")
+    fibres = lax.axis_size("fibre")
+    is_mid = jnp.logical_or(z == 1, z == 2)
+    is_end = jnp.logical_not(is_mid)
+    toward = jnp.where(z < 2, 1, -1)
+    inner = z + toward
+    outer = jnp.clip(z - toward, 0, 3)
+    tap_in = 1 + toward
+    tap_out = 1 - toward
+    has_low, has_high = f > 0, f < fibres - 1
+
+    weight_copies = [
+        pltpu.make_async_copy(cw_hbm.at[0], cw.at[0], w_sem.at[0]),
+        pltpu.make_async_copy(rs_hbm, rs, w_sem.at[1]),
+        pltpu.make_async_copy(cw_hbm.at[1], cw.at[1], w_sem.at[2]),
+        pltpu.make_async_copy(hd_hbm, hd, w_sem.at[3]),
+    ]
+    for c in weight_copies:
+        c.start()
+
+    barrier = pltpu.get_barrier_semaphore()
+
+    @pl.when(z > 0)
+    def _():
+        pl.semaphore_signal(barrier, inc=1, device_id={"tm": z - 1}, device_id_type=MESH)
+
+    @pl.when(z < 3)
+    def _():
+        pl.semaphore_signal(barrier, inc=1, device_id={"tm": z + 1}, device_id_type=MESH)
+
+    @pl.when(has_low)
+    def _():
+        pl.semaphore_signal(barrier, inc=1, device_id={"fibre": f - 1}, device_id_type=MESH)
+
+    @pl.when(has_high)
+    def _():
+        pl.semaphore_signal(barrier, inc=1, device_id={"fibre": f + 1}, device_id_type=MESH)
+
+    r_ids = lax.broadcasted_iota(jnp.int32, (rows, rows), 0)
+    c_ids = lax.broadcasted_iota(jnp.int32, (rows, rows), 1)
+    to_fibre_major = (
+        (r_ids % HALF) * strips + r_ids // HALF == c_ids
+    ).astype(jnp.float32).astype(jnp.bfloat16)
+    to_time_major = (
+        (c_ids % HALF) * strips + c_ids // HALF == r_ids
+    ).astype(jnp.float32).astype(jnp.bfloat16)
+
+    for h in range(halves):
+        chunk = x_ref[h * HALF:(h + 1) * HALF].reshape(rows, channels)
+        turned = jnp.dot(to_fibre_major, chunk, preferred_element_type=jnp.float32)
+        buf[M, h, 1:strips + 1] = turned.astype(jnp.bfloat16).reshape(strips, HALF, channels)
+
+    edge_zero = jnp.zeros((1, HALF, channels), jnp.bfloat16)
+
+    @pl.when(jnp.logical_not(has_low))
+    def _():
+        for k in (M, O, I, F, S1M, S1F):
+            for h in range(halves):
+                buf[k, h, 0:1] = edge_zero
+
+    @pl.when(jnp.logical_not(has_high))
+    def _():
+        for k in (M, O, I, F, S1M, S1F):
+            for h in range(halves):
+                buf[k, h, strips + 1:strips + 2] = edge_zero
+
+    pl.semaphore_wait(
+        barrier,
+        (z > 0).astype(jnp.int32) + (z < 3).astype(jnp.int32)
+        + has_low.astype(jnp.int32) + has_high.astype(jnp.int32),
+    )
+
+    def block_copy(src, dst, h, kind, to):
+        return pltpu.make_async_remote_copy(
+            src_ref=buf.at[src, h, pl.ds(1, strips)],
+            dst_ref=buf.at[dst, h, pl.ds(1, strips)],
+            send_sem=send_sem.at[kind, h],
+            recv_sem=recv_sem.at[dst, h],
+            device_id={"tm": to},
+            device_id_type=MESH,
+        )
+
+    def arrived(dst, h):
+        block_copy(dst, dst, h, 0, inner).wait_recv()
+
+    def halo_low(k, h):
+        return pltpu.make_async_remote_copy(
+            src_ref=buf.at[k, h, pl.ds(1, 1)],
+            dst_ref=buf.at[k, h, pl.ds(strips + 1, 1)],
+            send_sem=hsend.at[k, h, 0],
+            recv_sem=hrecv.at[k, h, 0],
+            device_id={"fibre": f - 1},
+            device_id_type=MESH,
+        )
+
+    def halo_high(k, h):
+        return pltpu.make_async_remote_copy(
+            src_ref=buf.at[k, h, pl.ds(strips, 1)],
+            dst_ref=buf.at[k, h, pl.ds(0, 1)],
+            send_sem=hsend.at[k, h, 1],
+            recv_sem=hrecv.at[k, h, 1],
+            device_id={"fibre": f + 1},
+            device_id_type=MESH,
+        )
+
+    def halo_start(k, h):
+        @pl.when(has_low)
+        def _():
+            halo_low(k, h).start()
+
+        @pl.when(has_high)
+        def _():
+            halo_high(k, h).start()
+
+    def halo_wait(k, h):
+        @pl.when(has_high)
+        def _():
+            halo_low(k, h).wait_recv()
+
+        @pl.when(has_low)
+        def _():
+            halo_high(k, h).wait_recv()
+
+    def halo_drain(k, h):
+        @pl.when(has_low)
+        def _():
+            halo_low(k, h).wait_send()
+
+        @pl.when(has_high)
+        def _():
+            halo_high(k, h).wait_send()
+
+    def gate(layer, taps, h):
+        total = cb_ref[layer]
+        for k, tap in taps:
+            views = [
+                buf[k, h, b:b + strips].reshape(rows, channels) for b in range(3)
+            ]
+            total = total + jnp.dot(
+                jnp.concatenate(views, axis=1), cw[layer, tap],
+                preferred_element_type=jnp.float32,
+            )
+        return (
+            jnp.tanh(total[:, :channels]) * jax.nn.sigmoid(total[:, channels:])
+        ).astype(jnp.bfloat16)
+
+    def first_layer(dst, centre, taps, h, own):
+        gated = gate(0, taps, h)
+        base = buf[centre, h, 1:strips + 1].reshape(rows, channels).astype(jnp.float32)
+        stream = base + jnp.dot(gated, rs[0, 0], preferred_element_type=jnp.float32)
+        buf[dst, h, 1:strips + 1] = stream.astype(jnp.bfloat16).reshape(strips, HALF, channels)
+        if own:
+            skip[h] = jnp.dot(gated, rs[1, 0], preferred_element_type=jnp.float32)
+
+    def last_layer(h):
+        gated = gate(1, ((S1M, 1), (S1F, tap_in)), h)
+        base = buf[S1M, h, 1:strips + 1].reshape(rows, channels).astype(jnp.float32)
+        stream = (
+            base + jnp.dot(gated, rs[0, 1], preferred_element_type=jnp.float32)
+        ).astype(jnp.bfloat16)
+        total = skip[h] + jnp.dot(gated, rs[1, 1], preferred_element_type=jnp.float32)
+        both = jnp.concatenate(
+            [stream, jnp.maximum(total, 0.0).astype(jnp.bfloat16)], axis=1
+        )
+        both = jnp.dot(
+            to_time_major, both, preferred_element_type=jnp.float32
+        ).astype(jnp.bfloat16)
+        res_ref[h * HALF:(h + 1) * HALF] = both[:, :channels].reshape(HALF, strips, channels)
+        out_ref[h * HALF:(h + 1) * HALF] = jnp.dot(
+            both[:, channels:], hd[...], preferred_element_type=jnp.float32
+        ).astype(jnp.bfloat16).reshape(HALF, strips, -1)
+
+    @pl.when(is_mid)
+    def _():
+        block_copy(M, I, 0, 0, inner).start()
+        block_copy(M, I, 0, 1, outer).start()
+        for h in range(halves):
+            halo_start(M, h)
+        block_copy(M, I, 1, 1, outer).start()
+        arrived(O, 0)
+        block_copy(O, F, 0, 2, inner).start()
+        block_copy(M, I, 1, 0, inner).start()
+        halo_start(O, 0)
+        arrived(I, 0)
+        halo_start(I, 0)
+        halo_wait(M, 0)
+        halo_wait(O, 0)
+        halo_wait(I, 0)
+        weight_copies[0].wait()
+        weight_copies[1].wait()
+        own_taps = ((O, tap_out), (M, 1), (I, tap_in))
+        first_layer(S1M, M, own_taps, 0, True)
+        halo_start(S1M, 0)
+        arrived(O, 1)
+        block_copy(O, F, 1, 2, inner).start()
+        halo_start(O, 1)
+        arrived(F, 0)
+        halo_start(F, 0)
+        halo_wait(F, 0)
+        inner_taps = ((M, tap_out), (I, 1), (F, tap_in))
+        first_layer(S1I, I, inner_taps, 0, False)
+        block_copy(S1I, S1F, 0, 3, outer).start()
+        far_taps = ((I, tap_out), (F, 1))
+        first_layer(S1F, F, far_taps, 0, False)
+        halo_start(S1F, 0)
+        arrived(I, 1)
+        halo_start(I, 1)
+        halo_wait(M, 1)
+        halo_wait(O, 1)
+        halo_wait(I, 1)
+        first_layer(S1M, M, own_taps, 1, True)
+        halo_start(S1M, 1)
+        halo_wait(S1M, 0)
+        halo_wait(S1F, 0)
+        weight_copies[2].wait()
+        weight_copies[3].wait()
+        last_layer(0)
+        arrived(F, 1)
+        halo_start(F, 1)
+        halo_wait(F, 1)
+        first_layer(S1I, I, inner_taps, 1, False)
+        block_copy(S1I, S1F, 1, 3, outer).start()
+        first_layer(S1F, F, far_taps, 1, False)
+        halo_start(S1F, 1)
+        halo_wait(S1M, 1)
+        halo_wait(S1F, 1)
+        last_layer(1)
+        for h in range(halves):
+            block_copy(M, I, h, 0, inner).wait_send()
+            block_copy(M, I, h, 1, outer).wait_send()
+            block_copy(O, F, h, 2, inner).wait_send()
+            block_copy(S1I, S1F, h, 3, outer).wait_send()
+            for k in (O, F):
+                halo_drain(k, h)
+
+    @pl.when(is_end)
+    def _():
+        for h in range(halves):
+            block_copy(M, O, h, 0, inner).start()
+        for h in range(halves):
+            halo_start(M, h)
+        weight_copies[0].wait()
+        weight_copies[1].wait()
+        for h in range(halves):
+            arrived(I, h)
+            halo_start(I, h)
+            halo_wait(M, h)
+            halo_wait(I, h)
+            first_layer(S1M, M, ((M, 1), (I, tap_in)), h, True)
+            halo_start(S1M, h)
+        weight_copies[2].wait()
+        weight_copies[3].wait()
+        for h in range(halves):
+            arrived(S1F, h)
+            halo_start(S1F, h)
+            halo_wait(S1M, h)
+            halo_wait(S1F, h)
+            last_layer(h)
+        for h in range(halves):
+            block_copy(M, O, h, 0, inner).wait_send()
+
+    for h in range(halves):
+        for k in (M, I, S1M, S1F):
+            halo_drain(k, h)
+
+
+def fused(recording, conv_weight, conv_bias, res_weight, skip_weight, head_weight):
+    times, strips, channels = recording.shape
+    layers = conv_weight.shape[0]
+    halves = times // HALF
+    pixels = head_weight.shape[1]
+    vmem = pl.BlockSpec(memory_space=pltpu.VMEM)
+    hbm = pl.BlockSpec(memory_space=pl.ANY)
+    weights = conv_weight.reshape(layers, 3, 3 * channels, 2 * channels)
+    sides = jnp.stack([res_weight, skip_weight])
+    return pl.pallas_call(
+        fused_kernel,
+        out_shape=(
+            jax.ShapeDtypeStruct((times, strips, channels), jnp.bfloat16),
+            jax.ShapeDtypeStruct((times, strips, pixels), jnp.bfloat16),
+        ),
+        in_specs=[vmem, hbm, vmem, hbm, hbm],
+        out_specs=(vmem, vmem),
+        scratch_shapes=[
+            pltpu.VMEM((7, halves, strips + 2, HALF, channels), jnp.bfloat16),
+            pltpu.VMEM(weights.shape, jnp.bfloat16),
+            pltpu.VMEM(sides.shape, jnp.bfloat16),
+            pltpu.VMEM(head_weight.shape, jnp.bfloat16),
+            pltpu.VMEM((halves, HALF * strips, channels), jnp.float32),
+            pltpu.SemaphoreType.DMA((4,)),
+            pltpu.SemaphoreType.DMA((4, halves)),
+            pltpu.SemaphoreType.DMA((7, halves)),
+            pltpu.SemaphoreType.DMA((7, halves, 2)),
+            pltpu.SemaphoreType.DMA((7, halves, 2)),
+        ],
+        compiler_params=pltpu.CompilerParams(
+            collective_id=0, has_side_effects=True, vmem_limit_bytes=56 * 2**20
+        ),
+        cost_estimate=pl.CostEstimate(
+            flops=10**10, bytes_accessed=10**7, transcendentals=10**6
+        ),
+    )(recording, weights, conv_bias.reshape(layers, 1, -1), sides, head_weight)
+
+
+def program(recording, conv_weight, *rest):
+    four = lax.axis_size("tm") == 4
+    if four and recording.shape[0] == DILATION_SPAN and conv_weight.shape[0] == 2:
+        return fused(recording, conv_weight, *rest)
+    return local(recording, conv_weight, *rest)
+
+
 def solution(mesh):
     return jax.shard_map(
-        local,
+        program,
         mesh=mesh,
         in_specs=(P(("groups", "tm"), "fibre", None), P(), P(), P(), P(), P()),
         out_specs=(P(("groups", "tm"), "fibre", None), P(("groups", "tm"), "fibre", None)),

time: 86.9 us -> 57.5 us (0.66)
  Pallas kernels: 0 us -> 48.4 us
  waiting for transfers between devices: 41 us -> 0 us
  starting transfers between devices: 22.4 us -> 0 us
  matrix products: 12.7 us -> 0 us
  other arithmetic: 3.72 us -> 1.87 us
    pallas_call x0 -> x1, Pallas kernels: none -> 48.4 us  [fused(): pl.pallas_call(fused_kernel, out_shape=(jax.ShapeDtypeStruct((times, stri...]
    ppermute x8 -> x0, waiting for transfers between devices: 41 us -> none  [the longest x4 34 us: passed_along(): return lax.ppermute(shard, axis, pairs)]
    ppermute x8 -> x0, starting transfers between devices: 22.4 us -> none  [the longest x4 11.1 us: passed_along(): return lax.ppermute(shard, axis, pairs)]
    dot_general x22 -> x0, matrix products: 12.7 us -> none  [the longest x18 8.83 us: gate_layer(): jnp.dot(receptive_view, layer_weight[time_offset, fibre_offset], preferre...]
    unnamed x10 -> x2, local copies, waits for them, and re-layouts: 0.51 us -> 5.05 us
    squeeze x3 -> x0, local copies, waits for them, and re-layouts: 3.1 us -> none  [the longest x1 2.84 us: local(): conv_weight[layer]]
    concatenate x2 -> x0, other arithmetic: 2.52 us -> none  [padded(): block = jnp.concatenate([low, block, high], axis=dim)]
    slice x6 -> x0, local copies, waits for them, and re-layouts: 2.24 us -> none  [the longest x5 2.23 us: gate_layer(): block[..., fibre_offset:fibre_offset + fibre_rows, :].reshape(-1, channels)]
  transfers between devices with their start and end apart: 8 -> 0, of which waited for: 6 -> 0; matrix products, arithmetic and copies ran while one was open for 4% -> 0% of each run, Pallas kernels for 0% -> 0%
where the time goes in v1:
time: 57.5 us; the launch traced here: 57.3 us
  Pallas kernels  48.4 us (84%)
  local copies, waits for them, and re-layouts  6.34 us (11%)
  other arithmetic  1.87 us (3%)
  between operations  0.64 us (1%)
    pallas_call x1, Pallas kernels, fused(): pl.pallas_call(fused_kernel, out_shape=(jax.ShapeDtypeStruct((times, stri...  48.4 us
    unnamed x2, local copies, waits for them, and re-layouts  5.05 us
    another operation x1, other arithmetic, fused(): sides = jnp.stack([res_weight, skip_weight])  1.87 us
    reshape x1, local copies, waits for them, and re-layouts, fused(): conv_bias.reshape(layers, 1, -1)  1.28 us

profile of v1, /device:TPU:1, one launch (start us, length us, event | category | flops | bytes accessed | tf_op | source)
XLA Modules:
  0.0 57.3 jit_solution(15588461928800847787)
XLA Ops:
  0.6 1.3 %reshape.11.cb_ref = f32[2,1,512]{2,1,0:T(1,128)} reshape(f32[2,512]{1,0:T(2,128)} %param.8) | data formatting | bytes 8192 | tf_op jit(solution)/shard_map/reshape | solution.py:399
  1.9 1.9 %pad_maximum_fusion.rs_hbm = bf16[2,2,256,256]{3,2,1,0:T(8,128)(2,1)} fusion(bf16[1,2,256,256]{3,2,1,0:T(8,128)(2,1)} %bitcast.3, bf16[1,2,256,256]{3,2,1,0:T(8,128)(2,1)} %bitcast.4), kind=kLoop, calls=%fused_computation | loop fusion | flops 262144 | bytes 1048576 | tf_op jit(solution)/shard_map/stack | solution.py:372
  3.8 48.4 %shard_map.77 = (bf16[32,32,256]{2,1,0:T(8,128)(2,1)}, bf16[32,32,1024]{2,1,0:T(8,128)(2,1)}) custom-call(bf16[32,32,256]{2,1,0:T(8,128)(2,1)} %x_ref.1, bf16[2,3,768,512]{3,2,1,0:T(8,128)(2,1)} %bitcast.5, f32[2,1,512]{2,1,0:T(1,128)} %reshape.11.cb_ref, bf16[2,2,256,256]{3,2,1,0:T(8,128)(2,1)} %pad_maximum_fusion.rs_hbm, bf16[256,1024]{1,0:T(8,128)(2,1)} %hd_hbm.1), custom_call_target="tpu_custom_call" | custom-call | flops 10000000000 | bytes 10000000 | tf_op jit(solution)/shard_map/pallas_call | solution.py:373
  52.2 1.9 %copy.10 = bf16[32,32,256]{2,1,0:T(8,128)(2,1)} copy(bf16[32,32,256]{2,1,0:T(8,128)(2,1)} %get-tuple-element.4) | data formatting | bytes 1048576
  54.1 3.2 %copy.11 = bf16[32,32,1024]{2,1,0:T(8,128)(2,1)} copy(bf16[32,32,1024]{2,1,0:T(8,128)(2,1)} %get-tuple-element.5) | data formatting | bytes 4194304

commit v2 on v1

--- a/solution.py
+++ b/solution.py
@@ -88,8 +88,10 @@
 HALF = 16
 
 
-def fused_kernel(x_ref, cw_hbm, cb_ref, rs_hbm, hd_hbm, res_ref, out_ref,
-                 buf, cw, rs, hd, skip, w_sem, send_sem, recv_sem, hsend, hrecv):
+def fused_kernel(x_hbm, cw_hbm, cb_hbm, rw_hbm, sw_hbm, stream_ref, rect_ref,
+                 x_ref, cb_ref, buf, cw, rw, sw, skip, w_sem, send_sem, recv_sem, hsend, hrecv):
+    x_copy = pltpu.make_async_copy(x_hbm, x_ref, w_sem.at[4])
+    x_copy.start()
     strips = x_ref.shape[1]
     channels = x_ref.shape[2]
     halves = x_ref.shape[0] // HALF
@@ -108,9 +110,10 @@
 
     weight_copies = [
         pltpu.make_async_copy(cw_hbm.at[0], cw.at[0], w_sem.at[0]),
-        pltpu.make_async_copy(rs_hbm, rs, w_sem.at[1]),
+        pltpu.make_async_copy(rw_hbm, rw, w_sem.at[1]),
         pltpu.make_async_copy(cw_hbm.at[1], cw.at[1], w_sem.at[2]),
-        pltpu.make_async_copy(hd_hbm, hd, w_sem.at[3]),
+        pltpu.make_async_copy(sw_hbm, sw, w_sem.at[3]),
+        pltpu.make_async_copy(cb_hbm, cb_ref, w_sem.at[5]),
     ]
     for c in weight_copies:
         c.start()
@@ -138,10 +141,8 @@
     to_fibre_major = (
         (r_ids % HALF) * strips + r_ids // HALF == c_ids
     ).astype(jnp.float32).astype(jnp.bfloat16)
-    to_time_major = (
-        (c_ids % HALF) * strips + c_ids // HALF == r_ids
-    ).astype(jnp.float32).astype(jnp.bfloat16)
-
+
+    x_copy.wait()
     for h in range(halves):
         chunk = x_ref[h * HALF:(h + 1) * HALF].reshape(rows, channels)
         turned = jnp.dot(to_fibre_major, chunk, preferred_element_type=jnp.float32)
@@ -228,7 +229,7 @@
             halo_high(k, h).wait_send()
 
     def gate(layer, taps, h):
-        total = cb_ref[layer]
+        total = cb_ref[layer:layer + 1]
         for k, tap in taps:
             views = [
                 buf[k, h, b:b + strips].reshape(rows, channels) for b in range(3)
@@ -244,28 +245,18 @@
     def first_layer(dst, centre, taps, h, own):
         gated = gate(0, taps, h)
         base = buf[centre, h, 1:strips + 1].reshape(rows, channels).astype(jnp.float32)
-        stream = base + jnp.dot(gated, rs[0, 0], preferred_element_type=jnp.float32)
+        stream = base + jnp.dot(gated, rw[0], preferred_element_type=jnp.float32)
         buf[dst, h, 1:strips + 1] = stream.astype(jnp.bfloat16).reshape(strips, HALF, channels)
         if own:
-            skip[h] = jnp.dot(gated, rs[1, 0], preferred_element_type=jnp.float32)
+            skip[h] = jnp.dot(gated, sw[0], preferred_element_type=jnp.float32)
 
     def last_layer(h):
         gated = gate(1, ((S1M, 1), (S1F, tap_in)), h)
         base = buf[S1M, h, 1:strips + 1].reshape(rows, channels).astype(jnp.float32)
-        stream = (
-            base + jnp.dot(gated, rs[0, 1], preferred_element_type=jnp.float32)
-        ).astype(jnp.bfloat16)
-        total = skip[h] + jnp.dot(gated, rs[1, 1], preferred_element_type=jnp.float32)
-        both = jnp.concatenate(
-            [stream, jnp.maximum(total, 0.0).astype(jnp.bfloat16)], axis=1
-        )
-        both = jnp.dot(
-            to_time_major, both, preferred_element_type=jnp.float32
-        ).astype(jnp.bfloat16)
-        res_ref[h * HALF:(h + 1) * HALF] = both[:, :channels].reshape(HALF, strips, channels)
-        out_ref[h * HALF:(h + 1) * HALF] = jnp.dot(
-            both[:, channels:], hd[...], preferred_element_type=jnp.float32
-        ).astype(jnp.bfloat16).reshape(HALF, strips, -1)
+        stream = base + jnp.dot(gated, rw[1], preferred_element_type=jnp.float32)
+        stream_ref[h] = stream.astype(jnp.bfloat16)
+        total = skip[h] + jnp.dot(gated, sw[1], preferred_element_type=jnp.float32)
+        rect_ref[h] = jnp.maximum(total, 0.0).astype(jnp.bfloat16)
 
     @pl.when(is_mid)
     def _():
@@ -285,6 +276,8 @@
         halo_wait(I, 0)
         weight_copies[0].wait()
         weight_copies[1].wait()
+        weight_copies[3].wait()
+        weight_copies[4].wait()
         own_taps = ((O, tap_out), (M, 1), (I, tap_in))
         first_layer(S1M, M, own_taps, 0, True)
         halo_start(S1M, 0)
@@ -310,7 +303,6 @@
         halo_wait(S1M, 0)
         halo_wait(S1F, 0)
         weight_copies[2].wait()
-        weight_copies[3].wait()
         last_layer(0)
         arrived(F, 1)
         halo_start(F, 1)
@@ -338,6 +330,8 @@
             halo_start(M, h)
         weight_copies[0].wait()
         weight_copies[1].wait()
+        weight_copies[3].wait()
+        weight_copies[4].wait()
         for h in range(halves):
             arrived(I, h)
             halo_start(I, h)
@@ -346,7 +340,6 @@
             first_layer(S1M, M, ((M, 1), (I, tap_in)), h, True)
             halo_start(S1M, h)
         weight_copies[2].wait()
-        weight_copies[3].wait()
         for h in range(halves):
             arrived(S1F, h)
             halo_start(S1F, h)
@@ -361,42 +354,80 @@
             halo_drain(k, h)
 
 
+def head_kernel(stream_ref, rect_ref, hd_ref, res_ref, out_ref):
+    times, strips, channels = res_ref.shape
+    rows = times * strips
+    r_ids = lax.broadcasted_iota(jnp.int32, (rows, rows), 0)
+    c_ids = lax.broadcasted_iota(jnp.int32, (rows, rows), 1)
+    to_time_major = (
+        (c_ids % HALF) * strips + c_ids // HALF == r_ids
+    ).astype(jnp.float32).astype(jnp.bfloat16)
+
+    def turned(block):
+        return jnp.dot(
+            to_time_major, block, preferred_element_type=jnp.float32
+        ).astype(jnp.bfloat16)
+
+    res_ref[...] = turned(stream_ref[0]).reshape(times, strips, channels)
+    out_ref[...] = jnp.dot(
+        turned(rect_ref[0]), hd_ref[...], preferred_element_type=jnp.float32
+    ).astype(jnp.bfloat16).reshape(times, strips, -1)
+
+
 def fused(recording, conv_weight, conv_bias, res_weight, skip_weight, head_weight):
     times, strips, channels = recording.shape
     layers = conv_weight.shape[0]
     halves = times // HALF
+    rows = HALF * strips
     pixels = head_weight.shape[1]
     vmem = pl.BlockSpec(memory_space=pltpu.VMEM)
     hbm = pl.BlockSpec(memory_space=pl.ANY)
     weights = conv_weight.reshape(layers, 3, 3 * channels, 2 * channels)
-    sides = jnp.stack([res_weight, skip_weight])
-    return pl.pallas_call(
+    flat = jax.ShapeDtypeStruct((halves, rows, channels), jnp.bfloat16)
+    stream, rectified = pl.pallas_call(
         fused_kernel,
-        out_shape=(
-            jax.ShapeDtypeStruct((times, strips, channels), jnp.bfloat16),
-            jax.ShapeDtypeStruct((times, strips, pixels), jnp.bfloat16),
-        ),
-        in_specs=[vmem, hbm, vmem, hbm, hbm],
+        out_shape=(flat, flat),
+        in_specs=[hbm] * 5,
         out_specs=(vmem, vmem),
         scratch_shapes=[
+            pltpu.VMEM(recording.shape, jnp.bfloat16),
+            pltpu.VMEM(conv_bias.shape, jnp.float32),
             pltpu.VMEM((7, halves, strips + 2, HALF, channels), jnp.bfloat16),
             pltpu.VMEM(weights.shape, jnp.bfloat16),
-            pltpu.VMEM(sides.shape, jnp.bfloat16),
-            pltpu.VMEM(head_weight.shape, jnp.bfloat16),
-            pltpu.VMEM((halves, HALF * strips, channels), jnp.float32),
-            pltpu.SemaphoreType.DMA((4,)),
+            pltpu.VMEM(res_weight.shape, jnp.bfloat16),
+            pltpu.VMEM(skip_weight.shape, jnp.bfloat16),
+            pltpu.VMEM((halves, rows, channels), jnp.float32),
+            pltpu.SemaphoreType.DMA((6,)),
             pltpu.SemaphoreType.DMA((4, halves)),
             pltpu.SemaphoreType.DMA((7, halves)),
             pltpu.SemaphoreType.DMA((7, halves, 2)),
             pltpu.SemaphoreType.DMA((7, halves, 2)),
         ],
         compiler_params=pltpu.CompilerParams(
-            collective_id=0, has_side_effects=True, vmem_limit_bytes=56 * 2**20
+            collective_id=0, has_side_effects=True, vmem_limit_bytes=62 * 2**20
         ),
         cost_estimate=pl.CostEstimate(
             flops=10**10, bytes_accessed=10**7, transcendentals=10**6
         ),
-    )(recording, weights, conv_bias.reshape(layers, 1, -1), sides, head_weight)
+    )(recording, weights, conv_bias, res_weight, skip_weight)
+    block = pl.BlockSpec((1, rows, channels), lambda h: (h, 0, 0))
+    return pl.pallas_call(
+        head_kernel,
+        grid=(halves,),
+        out_shape=(
+            jax.ShapeDtypeStruct((times, strips, channels), jnp.bfloat16),
+            jax.ShapeDtypeStruct((times, strips, pixels), jnp.bfloat16),
+        ),
+        in_specs=[block, block, pl.BlockSpec((channels, pixels), lambda h: (0, 0))],
+        out_specs=(
+            pl.BlockSpec((HALF, strips, channels), lambda h: (h, 0, 0)),
+            pl.BlockSpec((HALF, strips, pixels), lambda h: (h, 0, 0)),
+        ),
+        compiler_params=pltpu.CompilerParams(vmem_limit_bytes=62 * 2**20),
+        cost_estimate=pl.CostEstimate(
+            flops=10**9, bytes_accessed=4 * 10**6, transcendentals=0
+        ),
+    )(stream, rectified, head_weight)
 
 
 def program(recording, conv_weight, *rest):

time: 57.5 us -> 51.1 us (0.89)
  local copies, waits for them, and re-layouts: 6.34 us -> 0 us
  Pallas kernels: 48.4 us -> 50.3 us
  other arithmetic: 1.87 us -> 0 us
    unnamed x2 -> x0, local copies, waits for them, and re-layouts: 5.05 us -> none
    another operation x1 -> x0, other arithmetic: 1.87 us -> none  [fused(): sides = jnp.stack([res_weight, skip_weight])]
    pallas_call x1 -> x2, Pallas kernels: 48.4 us -> 50.3 us  [the longest x1 46.6 us: fused(): pl.pallas_call(fused_kernel, out_shape=(flat, flat), in_specs=[hbm] * 5,...]
    reshape x1 -> x0, local copies, waits for them, and re-layouts: 1.28 us -> none  [fused(): conv_bias.reshape(layers, 1, -1)]
where the time goes in v2:
time: 51.1 us; the launch traced here: 50.9 us
  Pallas kernels  50.3 us (98%)
  between operations  0.64 us (1%)
    pallas_call x1, Pallas kernels, fused(): pl.pallas_call(fused_kernel, out_shape=(flat, flat), in_specs=[hbm] * 5,...  46.6 us
    pallas_call x1, Pallas kernels, fused(): pl.pallas_call(head_kernel, grid=(halves,), out_shape=(jax.ShapeDtypeStru...  3.65 us

profile of v2, /device:TPU:1, one launch (start us, length us, event | category | flops | bytes accessed | tf_op | source)
XLA Modules:
  0.0 50.9 jit_solution(13736025430385198586)
XLA Ops:
  0.6 46.6 %shard_map.77 = (bf16[2,512,256]{2,1,0:T(8,128)(2,1)}, bf16[2,512,256]{2,1,0:T(8,128)(2,1)}) custom-call(bf16[32,32,256]{2,1,0:T(8,128)(2,1)} %x_hbm.1, bf16[2,3,768,512]{3,2,1,0:T(8,128)(2,1)} %bitcast.1, f32[2,512]{1,0:T(2,128)} %cb_hbm.1, bf16[2,256,256]{2,1,0:T(8,128)(2,1)} %rw_hbm.1, bf16[2,256,256]{2,1,0:T(8,128)(2,1)} %sw_hbm.1), custom_call_target="tpu_custom_call" | custom-call | flops 10000000000 | bytes 10000000 | tf_op jit(solution)/shard_map/pallas_call | solution.py:387
  47.3 3.7 %shard_map.78 = (bf16[32,32,256]{2,1,0:T(8,128)(2,1)}, bf16[32,32,1024]{2,1,0:T(8,128)(2,1)}) custom-call(bf16[2,512,256]{2,1,0:T(8,128)(2,1)} %get-tuple-element.4.stream_ref, bf16[2,512,256]{2,1,0:T(8,128)(2,1)} %get-tuple-element.5.rect_ref, bf16[256,1024]{1,0:T(8,128)(2,1)} %hd_ref.1), custom_call_target="tpu_custom_call" | custom-call | flops 1000000000 | bytes 4000000 | tf_op jit(solution)/shard_map/pallas_call | solution.py:414

commit v3 on v2

--- a/solution.py
+++ b/solution.py
@@ -168,18 +168,32 @@
         + has_low.astype(jnp.int32) + has_high.astype(jnp.int32),
     )
 
-    def block_copy(src, dst, h, kind, to):
+    def spans(kind):
+        edge = strips // 4 - (1 if kind == 3 else 0)
+        return ((0, edge), (strips - edge, strips), (edge, strips - edge))
+
+    def part_copy(src, dst, h, kind, to, part):
+        low, high = spans(kind)[part]
         return pltpu.make_async_remote_copy(
-            src_ref=buf.at[src, h, pl.ds(1, strips)],
-            dst_ref=buf.at[dst, h, pl.ds(1, strips)],
-            send_sem=send_sem.at[kind, h],
-            recv_sem=recv_sem.at[dst, h],
+            src_ref=buf.at[src, h, pl.ds(1 + low, high - low)],
+            dst_ref=buf.at[dst, h, pl.ds(1 + low, high - low)],
+            send_sem=send_sem.at[kind, h, part],
+            recv_sem=recv_sem.at[dst, h, part],
             device_id={"tm": to},
             device_id_type=MESH,
         )
 
-    def arrived(dst, h):
-        block_copy(dst, dst, h, 0, inner).wait_recv()
+    def send(src, dst, h, kind, to, parts=(0, 1, 2)):
+        for part in parts:
+            part_copy(src, dst, h, kind, to, part).start()
+
+    def drain(src, dst, h, kind, to):
+        for part in range(3):
+            part_copy(src, dst, h, kind, to, part).wait_send()
+
+    def arrived(dst, h, parts, kind=0):
+        for part in parts:
+            part_copy(dst, dst, h, kind, inner, part).wait_recv()
 
     def halo_low(k, h):
         return pltpu.make_async_remote_copy(
@@ -228,11 +242,12 @@
         def _():
             halo_high(k, h).wait_send()
 
-    def gate(layer, taps, h):
+    def gate(layer, taps, h, low, high):
         total = cb_ref[layer:layer + 1]
         for k, tap in taps:
             views = [
-                buf[k, h, b:b + strips].reshape(rows, channels) for b in range(3)
+                buf[k, h, b + low:b + high].reshape((high - low) * HALF, channels)
+                for b in range(3)
             ]
             total = total + jnp.dot(
                 jnp.concatenate(views, axis=1), cw[layer, tap],
@@ -242,112 +257,122 @@
             jnp.tanh(total[:, :channels]) * jax.nn.sigmoid(total[:, channels:])
         ).astype(jnp.bfloat16)
 
-    def first_layer(dst, centre, taps, h, own):
-        gated = gate(0, taps, h)
-        base = buf[centre, h, 1:strips + 1].reshape(rows, channels).astype(jnp.float32)
+    def first_layer(dst, centre, taps, h, own=False, span=(0, strips)):
+        low, high = span
+        gated = gate(0, taps, h, low, high)
+        base = buf[centre, h, 1 + low:1 + high].reshape(-1, channels).astype(jnp.float32)
         stream = base + jnp.dot(gated, rw[0], preferred_element_type=jnp.float32)
-        buf[dst, h, 1:strips + 1] = stream.astype(jnp.bfloat16).reshape(strips, HALF, channels)
+        buf[dst, h, 1 + low:1 + high] = stream.astype(jnp.bfloat16).reshape(
+            high - low, HALF, channels
+        )
         if own:
             skip[h] = jnp.dot(gated, sw[0], preferred_element_type=jnp.float32)
 
     def last_layer(h):
-        gated = gate(1, ((S1M, 1), (S1F, tap_in)), h)
+        gated = gate(1, ((S1M, 1), (S1F, tap_in)), h, 0, strips)
         base = buf[S1M, h, 1:strips + 1].reshape(rows, channels).astype(jnp.float32)
         stream = base + jnp.dot(gated, rw[1], preferred_element_type=jnp.float32)
         stream_ref[h] = stream.astype(jnp.bfloat16)
         total = skip[h] + jnp.dot(gated, sw[1], preferred_element_type=jnp.float32)
         rect_ref[h] = jnp.maximum(total, 0.0).astype(jnp.bfloat16)
 
+    edges, middle = (0, 1), (2,)
+
     @pl.when(is_mid)
     def _():
-        block_copy(M, I, 0, 0, inner).start()
-        block_copy(M, I, 0, 1, outer).start()
+        send(M, I, 0, 0, inner)
+        send(M, I, 0, 1, outer)
         for h in range(halves):
             halo_start(M, h)
-        block_copy(M, I, 1, 1, outer).start()
-        arrived(O, 0)
-        block_copy(O, F, 0, 2, inner).start()
-        block_copy(M, I, 1, 0, inner).start()
-        halo_start(O, 0)
-        arrived(I, 0)
+        send(M, I, 1, 1, outer)
+        for part in range(3):
+            arrived(O, 0, (part,))
+            send(O, F, 0, 2, inner, (part,))
+            if part == 1:
+                halo_start(O, 0)
+        send(M, I, 1, 0, inner)
+        arrived(I, 0, edges)
         halo_start(I, 0)
+        arrived(I, 0, middle)
         halo_wait(M, 0)
         halo_wait(O, 0)
         halo_wait(I, 0)
-        weight_copies[0].wait()
-        weight_copies[1].wait()
-        weight_copies[3].wait()
-        weight_copies[4].wait()
+        for c in (0, 1, 3, 4):
+            weight_copies[c].wait()
         own_taps = ((O, tap_out), (M, 1), (I, tap_in))
-        first_layer(S1M, M, own_taps, 0, True)
+        inner_taps = ((M, tap_out), (I, 1), (F, tap_in))
+        far_taps = ((I, tap_out), (F, 1))
+        first_layer(S1M, M, own_taps, 0, own=True)
         halo_start(S1M, 0)
-        arrived(O, 1)
-        block_copy(O, F, 1, 2, inner).start()
+        for part in range(3):
+            arrived(O, 1, (part,))
+            send(O, F, 1, 2, inner, (part,))
         halo_start(O, 1)
-        arrived(F, 0)
-        halo_start(F, 0)
-        halo_wait(F, 0)
-        inner_taps = ((M, tap_out), (I, 1), (F, tap_in))
-        first_layer(S1I, I, inner_taps, 0, False)
-        block_copy(S1I, S1F, 0, 3, outer).start()
-        far_taps = ((I, tap_out), (F, 1))
-        first_layer(S1F, F, far_taps, 0, False)
-        halo_start(S1F, 0)
-        arrived(I, 1)
+
+        def far_blocks(h):
+            arrived(F, h, edges)
+            halo_start(F, h)
+            halo_wait(F, h)
+            for part in edges:
+                first_layer(S1I, I, inner_taps, h, span=spans(3)[part])
+            send(S1I, S1F, h, 3, outer, edges)
+            arrived(F, h, middle)
+            first_layer(S1I, I, inner_taps, h, span=spans(3)[2])
+            send(S1I, S1F, h, 3, outer, middle)
+            first_layer(S1F, F, far_taps, h)
+            halo_start(S1F, h)
+
+        far_blocks(0)
+        arrived(I, 1, edges)
         halo_start(I, 1)
+        arrived(I, 1, middle)
         halo_wait(M, 1)
         halo_wait(O, 1)
         halo_wait(I, 1)
-        first_layer(S1M, M, own_taps, 1, True)
+        first_layer(S1M, M, own_taps, 1, own=True)
         halo_start(S1M, 1)
         halo_wait(S1M, 0)
         halo_wait(S1F, 0)
         weight_copies[2].wait()
         last_layer(0)
-        arrived(F, 1)
-        halo_start(F, 1)
-        halo_wait(F, 1)
-        first_layer(S1I, I, inner_taps, 1, False)
-        block_copy(S1I, S1F, 1, 3, outer).start()
-        first_layer(S1F, F, far_taps, 1, False)
-        halo_start(S1F, 1)
+        far_blocks(1)
         halo_wait(S1M, 1)
         halo_wait(S1F, 1)
         last_layer(1)
         for h in range(halves):
-            block_copy(M, I, h, 0, inner).wait_send()
-            block_copy(M, I, h, 1, outer).wait_send()
-            block_copy(O, F, h, 2, inner).wait_send()
-            block_copy(S1I, S1F, h, 3, outer).wait_send()
+            drain(M, I, h, 0, inner)
+            drain(M, I, h, 1, outer)
+            drain(O, F, h, 2, inner)
+            drain(S1I, S1F, h, 3, outer)
             for k in (O, F):
                 halo_drain(k, h)
 
     @pl.when(is_end)
     def _():
         for h in range(halves):
-            block_copy(M, O, h, 0, inner).start()
+            send(M, O, h, 0, inner)
         for h in range(halves):
             halo_start(M, h)
-        weight_copies[0].wait()
-        weight_copies[1].wait()
-        weight_copies[3].wait()
-        weight_copies[4].wait()
-        for h in range(halves):
-            arrived(I, h)
+        for c in (0, 1, 3, 4):
+            weight_copies[c].wait()
+        for h in range(halves):
+            arrived(I, h, edges)
             halo_start(I, h)
+            arrived(I, h, middle)
             halo_wait(M, h)
             halo_wait(I, h)
-            first_layer(S1M, M, ((M, 1), (I, tap_in)), h, True)
+            first_layer(S1M, M, ((M, 1), (I, tap_in)), h, own=True)
             halo_start(S1M, h)
         weight_copies[2].wait()
         for h in range(halves):
-            arrived(S1F, h)
+            arrived(S1F, h, edges, 3)
             halo_start(S1F, h)
+            arrived(S1F, h, middle, 3)
             halo_wait(S1M, h)
             halo_wait(S1F, h)
             last_layer(h)
         for h in range(halves):
-            block_copy(M, O, h, 0, inner).wait_send()
+            drain(M, O, h, 0, inner)
 
     for h in range(halves):
         for k in (M, I, S1M, S1F):
@@ -398,8 +423,8 @@
             pltpu.VMEM(skip_weight.shape, jnp.bfloat16),
             pltpu.VMEM((halves, rows, channels), jnp.float32),
             pltpu.SemaphoreType.DMA((6,)),
-            pltpu.SemaphoreType.DMA((4, halves)),
-            pltpu.SemaphoreType.DMA((7, halves)),
+            pltpu.SemaphoreType.DMA((4, halves, 3)),
+            pltpu.SemaphoreType.DMA((7, halves, 3)),
             pltpu.SemaphoreType.DMA((7, halves, 2)),
             pltpu.SemaphoreType.DMA((7, halves, 2)),
         ],

time: 51.1 us -> 44.7 us (0.87)
  Pallas kernels: 50.3 us -> 43.9 us
    pallas_call x1, Pallas kernels: 46.6 us -> 40.3 us  [fused(): pl.pallas_call(fused_kernel, out_shape=(flat, flat), in_specs=[hbm] * 5,...]
where the time goes in v3:
time: 44.7 us; the launch traced here: 44.5 us
  Pallas kernels  43.9 us (98%)
  between operations  0.64 us (1%)
    pallas_call x1, Pallas kernels, fused(): pl.pallas_call(fused_kernel, out_shape=(flat, flat), in_specs=[hbm] * 5,...  40.3 us
    pallas_call x1, Pallas kernels, fused(): pl.pallas_call(head_kernel, grid=(halves,), out_shape=(jax.ShapeDtypeStru...  3.65 us

profile of v3, /device:TPU:1, one launch (start us, length us, event | category | flops | bytes accessed | tf_op | source)
XLA Modules:
  0.0 44.5 jit_solution(17766498865636079207)
XLA Ops:
  0.6 40.3 %shard_map.77 = (bf16[2,512,256]{2,1,0:T(8,128)(2,1)}, bf16[2,512,256]{2,1,0:T(8,128)(2,1)}) custom-call(bf16[32,32,256]{2,1,0:T(8,128)(2,1)} %x_hbm.1, bf16[2,3,768,512]{3,2,1,0:T(8,128)(2,1)} %bitcast.1, f32[2,512]{1,0:T(2,128)} %cb_hbm.1, bf16[2,256,256]{2,1,0:T(8,128)(2,1)} %rw_hbm.1, bf16[2,256,256]{2,1,0:T(8,128)(2,1)} %sw_hbm.1), custom_call_target="tpu_custom_call" | custom-call | flops 10000000000 | bytes 10000000 | tf_op jit(solution)/shard_map/pallas_call | solution.py:412
  40.9 3.7 %shard_map.78 = (bf16[32,32,256]{2,1,0:T(8,128)(2,1)}, bf16[32,32,1024]{2,1,0:T(8,128)(2,1)}) custom-call(bf16[2,512,256]{2,1,0:T(8,128)(2,1)} %get-tuple-element.4.stream_ref, bf16[2,512,256]{2,1,0:T(8,128)(2,1)} %get-tuple-element.5.rect_ref, bf16[256,1024]{1,0:T(8,128)(2,1)} %hd_ref.1), custom_call_target="tpu_custom_call" | custom-call | flops 1000000000 | bytes 4000000 | tf_op jit(solution)/shard_map/pallas_call | solution.py:439

commit v4 on v3

--- a/solution.py
+++ b/solution.py
@@ -89,7 +89,7 @@
 
 
 def fused_kernel(x_hbm, cw_hbm, cb_hbm, rw_hbm, sw_hbm, stream_ref, rect_ref,
-                 x_ref, cb_ref, buf, cw, rw, sw, skip, w_sem, send_sem, recv_sem, hsend, hrecv):
+                 x_ref, cb_ref, buf, cw, rw, sw, skip, partial, w_sem, send_sem, recv_sem, hsend, hrecv):
     x_copy = pltpu.make_async_copy(x_hbm, x_ref, w_sem.at[4])
     x_copy.start()
     strips = x_ref.shape[1]
@@ -242,8 +242,7 @@
         def _():
             halo_high(k, h).wait_send()
 
-    def gate(layer, taps, h, low, high):
-        total = cb_ref[layer:layer + 1]
+    def added(total, layer, taps, h, low, high):
         for k, tap in taps:
             views = [
                 buf[k, h, b + low:b + high].reshape((high - low) * HALF, channels)
@@ -253,13 +252,24 @@
                 jnp.concatenate(views, axis=1), cw[layer, tap],
                 preferred_element_type=jnp.float32,
             )
+        return total
+
+    def prepare(slot, layer, taps, h):
+        partial[slot] = added(cb_ref[layer:layer + 1], layer, taps, h, 0, strips)
+
+    def gate(layer, taps, h, low, high, slot=None):
+        if slot is None:
+            total = cb_ref[layer:layer + 1]
+        else:
+            total = partial[slot, low * HALF:high * HALF]
+        total = added(total, layer, taps, h, low, high)
         return (
             jnp.tanh(total[:, :channels]) * jax.nn.sigmoid(total[:, channels:])
         ).astype(jnp.bfloat16)
 
-    def first_layer(dst, centre, taps, h, own=False, span=(0, strips)):
+    def first_layer(dst, centre, taps, h, own=False, span=(0, strips), slot=None):
         low, high = span
-        gated = gate(0, taps, h, low, high)
+        gated = gate(0, taps, h, low, high, slot)
         base = buf[centre, h, 1 + low:1 + high].reshape(-1, channels).astype(jnp.float32)
         stream = base + jnp.dot(gated, rw[0], preferred_element_type=jnp.float32)
         buf[dst, h, 1 + low:1 + high] = stream.astype(jnp.bfloat16).reshape(
@@ -269,7 +279,7 @@
             skip[h] = jnp.dot(gated, sw[0], preferred_element_type=jnp.float32)
 
     def last_layer(h):
-        gated = gate(1, ((S1M, 1), (S1F, tap_in)), h, 0, strips)
+        gated = gate(1, ((S1F, tap_in),), h, 0, strips, 2)
         base = buf[S1M, h, 1:strips + 1].reshape(rows, channels).astype(jnp.float32)
         stream = base + jnp.dot(gated, rw[1], preferred_element_type=jnp.float32)
         stream_ref[h] = stream.astype(jnp.bfloat16)
@@ -300,8 +310,8 @@
         for c in (0, 1, 3, 4):
             weight_copies[c].wait()
         own_taps = ((O, tap_out), (M, 1), (I, tap_in))
-        inner_taps = ((M, tap_out), (I, 1), (F, tap_in))
-        far_taps = ((I, tap_out), (F, 1))
+        inner_taps = ((F, tap_in),)
+        far_taps = ((F, 1),)
         first_layer(S1M, M, own_taps, 0, own=True)
         halo_start(S1M, 0)
         for part in range(3):
@@ -310,16 +320,18 @@
         halo_start(O, 1)
 
         def far_blocks(h):
+            prepare(0, 0, ((M, tap_out), (I, 1)), h)
+            prepare(1, 0, ((I, tap_out),), h)
             arrived(F, h, edges)
             halo_start(F, h)
             halo_wait(F, h)
             for part in edges:
-                first_layer(S1I, I, inner_taps, h, span=spans(3)[part])
+                first_layer(S1I, I, inner_taps, h, span=spans(3)[part], slot=0)
             send(S1I, S1F, h, 3, outer, edges)
             arrived(F, h, middle)
-            first_layer(S1I, I, inner_taps, h, span=spans(3)[2])
+            first_layer(S1I, I, inner_taps, h, span=spans(3)[2], slot=0)
             send(S1I, S1F, h, 3, outer, middle)
-            first_layer(S1F, F, far_taps, h)
+            first_layer(S1F, F, far_taps, h, slot=1)
             halo_start(S1F, h)
 
         far_blocks(0)
@@ -334,9 +346,11 @@
         halo_wait(S1M, 0)
         halo_wait(S1F, 0)
         weight_copies[2].wait()
+        prepare(2, 1, ((S1M, 1),), 0)
         last_layer(0)
+        halo_wait(S1M, 1)
+        prepare(2, 1, ((S1M, 1),), 1)
         far_blocks(1)
-        halo_wait(S1M, 1)
         halo_wait(S1F, 1)
         last_layer(1)
         for h in range(halves):
@@ -365,10 +379,11 @@
             halo_start(S1M, h)
         weight_copies[2].wait()
         for h in range(halves):
+            halo_wait(S1M, h)
+            prepare(2, 1, ((S1M, 1),), h)
             arrived(S1F, h, edges, 3)
             halo_start(S1F, h)
             arrived(S1F, h, middle, 3)
-            halo_wait(S1M, h)
             halo_wait(S1F, h)
             last_layer(h)
         for h in range(halves):
@@ -422,6 +437,7 @@
             pltpu.VMEM(res_weight.shape, jnp.bfloat16),
             pltpu.VMEM(skip_weight.shape, jnp.bfloat16),
             pltpu.VMEM((halves, rows, channels), jnp.float32),
+            pltpu.VMEM((3, rows, 2 * channels), jnp.float32),
             pltpu.SemaphoreType.DMA((6,)),
             pltpu.SemaphoreType.DMA((4, halves, 3)),
             pltpu.SemaphoreType.DMA((7, halves, 3)),

time: 44.7 us -> 47.2 us (1.056)
  Pallas kernels: 43.9 us -> 46.1 us
    pallas_call x1, Pallas kernels: 40.3 us -> 42.4 us  [fused(): pl.pallas_call(fused_kernel, out_shape=(flat, flat), in_specs=[hbm] * 5,...]
where the time goes in v4:
time: 47.2 us; the launch traced here: 46.7 us
  Pallas kernels  46.1 us (98%)
  between operations  0.64 us (1%)
    pallas_call x1, Pallas kernels, fused(): pl.pallas_call(fused_kernel, out_shape=(flat, flat), in_specs=[hbm] * 5,...  42.4 us
    pallas_call x1, Pallas kernels, fused(): pl.pallas_call(head_kernel, grid=(halves,), out_shape=(jax.ShapeDtypeStru...  3.65 us

profile of v4, /device:TPU:1, one launch (start us, length us, event | category | flops | bytes accessed | tf_op | source)
XLA Modules:
  0.0 46.7 jit_solution(13295113111259644753)
XLA Ops:
  0.6 42.4 %shard_map.77 = (bf16[2,512,256]{2,1,0:T(8,128)(2,1)}, bf16[2,512,256]{2,1,0:T(8,128)(2,1)}) custom-call(bf16[32,32,256]{2,1,0:T(8,128)(2,1)} %x_hbm.1, bf16[2,3,768,512]{3,2,1,0:T(8,128)(2,1)} %bitcast.1, f32[2,512]{1,0:T(2,128)} %cb_hbm.1, bf16[2,256,256]{2,1,0:T(8,128)(2,1)} %rw_hbm.1, bf16[2,256,256]{2,1,0:T(8,128)(2,1)} %sw_hbm.1), custom_call_target="tpu_custom_call" | custom-call | flops 10000000000 | bytes 10000000 | tf_op jit(solution)/shard_map/pallas_call | solution.py:427
  43.1 3.7 %shard_map.78 = (bf16[32,32,256]{2,1,0:T(8,128)(2,1)}, bf16[32,32,1024]{2,1,0:T(8,128)(2,1)}) custom-call(bf16[2,512,256]{2,1,0:T(8,128)(2,1)} %get-tuple-element.4.stream_ref, bf16[2,512,256]{2,1,0:T(8,128)(2,1)} %get-tuple-element.5.rect_ref, bf16[256,1024]{1,0:T(8,128)(2,1)} %hd_ref.1), custom_call_target="tpu_custom_call" | custom-call | flops 1000000000 | bytes 4000000 | tf_op jit(solution)/shard_map/pallas_call | solution.py:455

commit v5 on v3

--- a/solution.py
+++ b/solution.py
@@ -89,9 +89,15 @@
 
 
 def fused_kernel(x_hbm, cw_hbm, cb_hbm, rw_hbm, sw_hbm, stream_ref, rect_ref,
-                 x_ref, cb_ref, buf, cw, rw, sw, skip, w_sem, send_sem, recv_sem, hsend, hrecv):
-    x_copy = pltpu.make_async_copy(x_hbm, x_ref, w_sem.at[4])
-    x_copy.start()
+                 x_ref, cb_ref, buf, cw, rw, sw, skip, x_sem, w_sem, send_sem, recv_sem, hsend, hrecv):
+    x_copies = [
+        pltpu.make_async_copy(
+            x_hbm.at[pl.ds(h * HALF, HALF)], x_ref.at[pl.ds(h * HALF, HALF)], x_sem.at[h]
+        )
+        for h in range(x_ref.shape[0] // HALF)
+    ]
+    for c in x_copies:
+        c.start()
     strips = x_ref.shape[1]
     channels = x_ref.shape[2]
     halves = x_ref.shape[0] // HALF
@@ -137,16 +143,18 @@
         pl.semaphore_signal(barrier, inc=1, device_id={"fibre": f + 1}, device_id_type=MESH)
 
     r_ids = lax.broadcasted_iota(jnp.int32, (rows, rows), 0)
-    c_ids = lax.broadcasted_iota(jnp.int32, (rows, rows), 1)
+    c_ids = lax.broadcasted_iota(jnp.int32, (1, rows), 1)
     to_fibre_major = (
-        (r_ids % HALF) * strips + r_ids // HALF == c_ids
+        (c_ids % strips) * HALF + c_ids // strips == r_ids
     ).astype(jnp.float32).astype(jnp.bfloat16)
 
-    x_copy.wait()
-    for h in range(halves):
+    def turn(h):
+        x_copies[h].wait()
         chunk = x_ref[h * HALF:(h + 1) * HALF].reshape(rows, channels)
         turned = jnp.dot(to_fibre_major, chunk, preferred_element_type=jnp.float32)
         buf[M, h, 1:strips + 1] = turned.astype(jnp.bfloat16).reshape(strips, HALF, channels)
+
+    turn(0)
 
     edge_zero = jnp.zeros((1, HALF, channels), jnp.bfloat16)
 
@@ -282,6 +290,7 @@
     def _():
         send(M, I, 0, 0, inner)
         send(M, I, 0, 1, outer)
+        turn(1)
         for h in range(halves):
             halo_start(M, h)
         send(M, I, 1, 1, outer)
@@ -349,8 +358,9 @@
 
     @pl.when(is_end)
     def _():
-        for h in range(halves):
-            send(M, O, h, 0, inner)
+        send(M, O, 0, 0, inner)
+        turn(1)
+        send(M, O, 1, 0, inner)
         for h in range(halves):
             halo_start(M, h)
         for c in (0, 1, 3, 4):
@@ -383,7 +393,7 @@
     times, strips, channels = res_ref.shape
     rows = times * strips
     r_ids = lax.broadcasted_iota(jnp.int32, (rows, rows), 0)
-    c_ids = lax.broadcasted_iota(jnp.int32, (rows, rows), 1)
+    c_ids = lax.broadcasted_iota(jnp.int32, (1, rows), 1)
     to_time_major = (
         (c_ids % HALF) * strips + c_ids // HALF == r_ids
     ).astype(jnp.float32).astype(jnp.bfloat16)
@@ -422,6 +432,7 @@
             pltpu.VMEM(res_weight.shape, jnp.bfloat16),
             pltpu.VMEM(skip_weight.shape, jnp.bfloat16),
             pltpu.VMEM((halves, rows, channels), jnp.float32),
+            pltpu.SemaphoreType.DMA((halves,)),
             pltpu.SemaphoreType.DMA((6,)),
             pltpu.SemaphoreType.DMA((4, halves, 3)),
             pltpu.SemaphoreType.DMA((7, halves, 3)),

time: 44.7 us -> 46 us (1.029)
  Pallas kernels: 43.9 us -> 45.2 us
    pallas_call x1, Pallas kernels: 40.3 us -> 41.5 us  [fused(): pl.pallas_call(fused_kernel, out_shape=(flat, flat), in_specs=[hbm] * 5,...]
where the time goes in v5:
time: 46 us; the launch traced here: 45.8 us
  Pallas kernels  45.2 us (98%)
  between operations  0.64 us (1%)
    pallas_call x1, Pallas kernels, fused(): pl.pallas_call(fused_kernel, out_shape=(flat, flat), in_specs=[hbm] * 5,...  41.5 us
    pallas_call x1, Pallas kernels, fused(): pl.pallas_call(head_kernel, grid=(halves,), out_shape=(jax.ShapeDtypeStru...  3.65 us

profile of v5, /device:TPU:1, one launch (start us, length us, event | category | flops | bytes accessed | tf_op | source)
XLA Modules:
  0.0 45.8 jit_solution(12440888605961583689)
XLA Ops:
  0.6 41.5 %shard_map.77 = (bf16[2,512,256]{2,1,0:T(8,128)(2,1)}, bf16[2,512,256]{2,1,0:T(8,128)(2,1)}) custom-call(bf16[32,32,256]{2,1,0:T(8,128)(2,1)} %x_hbm.1, bf16[2,3,768,512]{3,2,1,0:T(8,128)(2,1)} %bitcast.1, f32[2,512]{1,0:T(2,128)} %cb_hbm.1, bf16[2,256,256]{2,1,0:T(8,128)(2,1)} %rw_hbm.1, bf16[2,256,256]{2,1,0:T(8,128)(2,1)} %sw_hbm.1), custom_call_target="tpu_custom_call" | custom-call | flops 10000000000 | bytes 10000000 | tf_op jit(solution)/shard_map/pallas_call | solution.py:422
  42.2 3.7 %shard_map.78 = (bf16[32,32,256]{2,1,0:T(8,128)(2,1)}, bf16[32,32,1024]{2,1,0:T(8,128)(2,1)}) custom-call(bf16[2,512,256]{2,1,0:T(8,128)(2,1)} %get-tuple-element.4.stream_ref, bf16[2,512,256]{2,1,0:T(8,128)(2,1)} %get-tuple-element.5.rect_ref, bf16[256,1024]{1,0:T(8,128)(2,1)} %hd_ref.1), custom_call_target="tpu_custom_call" | custom-call | flops 1000000000 | bytes 4000000 | tf_op jit(solution)/shard_map/pallas_call | solution.py:450
